TPU v7x, 256 devices: a whole 4x4x8 slice. The times are simulated.
256 devices in a mesh: grp: 16 (over x_hi, y, core), sub: 16 (over z, x_lo).
Axes of the slice: x: 4 (x_hi: 2, x_lo: 2; x = x_hi * 2 + x_lo), y: 4, z: 8, core: 2. Of those that a mesh axis runs over, the one named last changes fastest.
Arguments:
- basis: bfloat16 [16, 16, 270, 1152], P('grp', 'sub'), may hold values from -6 to 6
- stiffness: bfloat16 [16, 16, 1152, 1152], P('grp', 'sub'), may hold values from -0.1875 to 0.1875
- inverse: bfloat16 [16, 16, 1152, 1152], P('grp', 'sub'), may hold values from -0.1875 to 0.1875
- coupling: bfloat16 [16, 16, 4, 768, 1152], P('grp', 'sub'), may hold values from -0.109375 to 0.109375
- panel_index: int32 [16, 16, 4, 6], P('grp', 'sub'), may hold values from 0 to 8, as said below
- panel_count: int32 [16, 16, 4], P('grp', 'sub'), may hold values from 1 to 6, as said below
- owner_map: int32 [16, 16, 270], P('grp', 'sub'), may hold values from 0 to 2047, as said below
Outputs:
- coarse_matrix: float32 [2048, 2048], P(('grp', 'sub'))
Inputs may be any that keep to these rules, and one draw needn't show every extreme that they name: `panel_index`: in every draw some slot names panel 9 - 1 and some names panel 0. `panel_count`: in every draw some direction has 6 live slots and some has one. Subdomain (g, s) owns the rows b * 8 to b * 8 + 7 of coarse_matrix with b = g * 16 + s; entries of owner_map may name any column, repeats allowed; column 0 and column 2048 - 1 are named in every draw.
All inputs are finite; a program needn't handle non-finite values.
Results may differ from a plain program's by a relative error of at most 0.0056.
Values may be sent and summed in bfloat16 or wider, within the bound.
A program may use at most 128 MiB of HBM per device.

v0:
```python
import jax
import jax.numpy as jnp
from jax import lax
from jax.sharding import Mesh
from jax.sharding import PartitionSpec as P

K = 270
PANEL = 128
NB = 9
CMAX = 6
OWN = 8
GRP_SUB = ("grp", "sub_0", "sub_1")
SUB = ("sub_0", "sub_1")


def extended(block, sides, width):
    for axis, dim in sides:
        count = lax.axis_size(axis)
        forward = [(i, i + 1) for i in range(count - 1)]
        backward = [(target, source) for source, target in forward]
        low = lax.ppermute(
            lax.slice_in_dim(block, block.shape[dim] - width, None, axis=dim), axis, forward
        )
        high = lax.ppermute(lax.slice_in_dim(block, 0, width, axis=dim), axis, backward)
        block = jnp.concatenate([low, block, high], axis=dim)
    return block


def summed_rows(shard, axes, dim):
    for axis in axes:
        shard = lax.psum_scatter(shard, axis, scatter_dimension=dim, tiled=True)
    return shard


def split_up(shard, dim, size):
    before, after = (shard.shape[:dim], shard.shape[dim + 1 :])
    return jnp.moveaxis(shard.reshape(*before, size, -1, *after), dim, 0)


def sum_at_owner(shard, axis, dim):
    size = lax.axis_size(axis)
    pieces = lax.all_to_all(split_up(shard, dim, size), axis, 0, 0, tiled=True)
    return jnp.sum(pieces, axis=0)


def live_slots(values, live_count):
    alive_mask = (jnp.arange(CMAX) < live_count).astype(values.dtype)
    return values.reshape(K, CMAX, PANEL) * alive_mask[None, :, None]


def select_panels(values, panel_ids):
    panels = values.reshape(K, NB, PANEL)
    picker = (panel_ids[:, None] == jnp.arange(NB, dtype=jnp.int32)[None, :]).astype(jnp.bfloat16)
    chosen = jnp.einsum("knp,cn->kcp", panels, picker, preferred_element_type=jnp.float32)
    return chosen.astype(jnp.bfloat16)


def spread_block(coarse, rows_at, cols_at, columns_all):
    positions = jnp.arange(columns_all, dtype=jnp.int32)
    row_table = (rows_at[:, None] == positions[None, :]).astype(jnp.float32)
    col_table = (cols_at[:, None] == positions[None, :]).astype(jnp.float32)
    placed_rows = lax.dot_general(
        row_table,
        coarse,
        (((0,), (0,)), ((), ())),
        precision=lax.Precision.HIGHEST,
        preferred_element_type=jnp.float32,
    )
    return jnp.dot(
        placed_rows, col_table, precision=lax.Precision.HIGHEST, preferred_element_type=jnp.float32
    )


def shards(basis, stiffness, inverse, coupling, panel_index, panel_count, owner_map):
    basis_local = basis[0, 0]
    stiffness_local = stiffness[0, 0]
    inverse_local = inverse[0, 0]
    coupling_local = coupling[0, 0]
    index_local = panel_index[0, 0]
    count_local = panel_count[0, 0]
    owner_local = owner_map[0, 0]
    rows_device = NB * PANEL
    slot_width = CMAX * PANEL
    grp_part = index_local[0:2]
    sub_part = index_local[2:4]
    request = jnp.concatenate(
        [
            jnp.broadcast_to(grp_part[:, None, :], (2, 2, CMAX)),
            jnp.broadcast_to(sub_part[None, :, :], (2, 2, CMAX)),
        ],
        axis=2,
    )
    requested = extended(request, (("grp", 0), (SUB, 1)), 1)

    def pack_panels(wanted):
        return select_panels(basis_local, wanted).reshape(K, slot_width)

    grp_out = jnp.concatenate(
        [pack_panels(requested[0, 1, :CMAX]), pack_panels(requested[3, 1, :CMAX])], axis=1
    )
    sub_out = jnp.concatenate(
        [pack_panels(requested[1, 0, CMAX:]), pack_panels(requested[1, 3, CMAX:])], axis=1
    )
    grp_in = extended(grp_out, (("grp", 1),), slot_width)
    sub_in = extended(sub_out, ((SUB, 1),), slot_width)
    arrived = [
        grp_in[:, :slot_width],
        grp_in[:, 3 * slot_width :],
        sub_in[:, :slot_width],
        sub_in[:, 3 * slot_width :],
    ]
    picked = [live_slots(arrived[direction], count_local[direction]) for direction in range(4)]
    rows_margin = jnp.stack(picked, axis=1).reshape(K, 4 * slot_width)
    margin = jnp.dot(
        rows_margin,
        coupling_local.reshape(4 * slot_width, rows_device),
        preferred_element_type=jnp.float32,
    ).astype(jnp.bfloat16)
    extension = (
        jnp.dot(basis_local, inverse_local, preferred_element_type=jnp.float32)
        + jnp.dot(margin, inverse_local, preferred_element_type=jnp.float32)
    ).astype(jnp.bfloat16)
    projected = jnp.dot(extension, stiffness_local, preferred_element_type=jnp.float32).astype(
        jnp.bfloat16
    )
    scale_factor = float(NB * PANEL * K) ** (-0.5)
    coarse = jnp.dot(projected, extension.T, preferred_element_type=jnp.float32) * scale_factor
    group_count = lax.axis_size("grp")
    member_count = lax.axis_size(SUB)
    columns_all = OWN * group_count * member_count
    owner_block = owner_local // OWN
    offset = owner_local % OWN
    row_place = (
        owner_block % member_count * group_count + owner_block // member_count
    ) * OWN + offset
    contributions = spread_block(coarse, row_place, owner_local, columns_all)
    sectioned = summed_rows(contributions, SUB, 0)
    owned_block = sum_at_owner(sectioned, "grp", 0)
    return owned_block


def solution(mesh):
    split = Mesh(mesh.devices.reshape(mesh.shape["grp"], 8, 2), ("grp", "sub_0", "sub_1"))
    in_specs = (
        P("grp", SUB, None, None),
        P("grp", SUB, None, None),
        P("grp", SUB, None, None),
        P("grp", SUB, None, None, None),
        P("grp", SUB, None, None),
        P("grp", SUB, None),
        P("grp", SUB, None),
    )
    out_specs = P(GRP_SUB, None)
    return jax.shard_map(
        shards, mesh=split, in_specs=in_specs, out_specs=out_specs, check_vma=False
    )
```

profile of v0, /device:TPU:25, one launch (start us, length us, event | category | flops | bytes accessed | tf_op | source)
XLA Modules:
  0.0 363.7 jit_solution(201940436425656460)
XLA Ops:
  8.0 4.9 %collective-permute-start.2 = (s32[1,2,12]{2,1,0:T(2,128)}, s32[1,2,12]{2,1,0:T(2,128)}, u32[]{:S(2)}, u32[]{:S(2)}) collective-permute-start(s32[1,2,12]{2,1,0:T(2,128)} %get-tuple-element.7), channel_id=1, source_target_pairs={{0,16},{16,32},{32,48},{48,64},{64,80},{80,96},{96,112},{112,128},... | collective-permute-start | bytes 296 | tf_op jit(solution)/shard_map/ppermute | solution.py:21
  12.9 1.9 collective-permute-start
  21.7 1.5 copy.8
  23.2 3.2 fusion.3
  26.4 1.9 copy.9
  30.5 4.0 %collective-permute-start.6 = (s32[4,1,12]{2,1,0:T(1,128)S(1)}, s32[4,1,12]{2,1,0:T(1,128)S(1)}, u32[]{:S(2)}, u32[]{:S(2)}) collective-permute-start(s32[4,1,12]{2,1,0:T(1,128)S(1)} %get-tuple-element.6), channel_id=1, source_target_pairs={{0,1},{1,2},{2,3},{3,4},{4,5},{5,6},{6,7},{7,8},{8,9},{9,10},{10,1... | collective-permute-start | bytes 584 | tf_op jit(solution)/shard_map/ppermute | solution.py:21
  35.1 1.6 fusion.14
  38.9 1.9 collective-permute-start.3
  40.8 7.8 %collective-permute-start.1 = (bf16[270,768]{1,0:T(8,128)(2,1)}, bf16[270,768]{1,0:T(8,128)(2,1)}, u32[]{:S(2)}, u32[]{:S(2)}) collective-permute-start(bf16[270,768]{1,0:T(8,128)(2,1)} %bitcast.26), channel_id=1, source_target_pairs={{0,16},{16,32},{32,48},{48,64},{64,80},{80,96},{96,112},{112,128},... | collective-permute-start | bytes 1244168 | tf_op jit(solution)/shard_map/ppermute | solution.py:21
  52.7 4.7 %collective-permute-start.5 = (bf16[270,768]{1,0:T(8,128)(2,1)}, bf16[270,768]{1,0:T(8,128)(2,1)}, u32[]{:S(2)}, u32[]{:S(2)}) collective-permute-start(bf16[270,768]{1,0:T(8,128)(2,1)} %bitcast.32), channel_id=1, source_target_pairs={{0,1},{1,2},{2,3},{3,4},{4,5},{5,6},{6,7},{7,8},{8,9},{9,10},{10,1... | collective-permute-start | bytes 1244168 | tf_op jit(solution)/shard_map/ppermute | solution.py:21
  58.9 6.9 %collective-permute-done.1 = bf16[270,768]{1,0:T(8,128)(2,1)} collective-permute-done((bf16[270,768]{1,0:T(8,128)(2,1)}, bf16[270,768]{1,0:T(8,128)(2,1)}, u32[]{:S(2)}, u32[]{:S(2)}) %collective-permute-start.1) | collective-permute-done | bytes 414752 | tf_op jit(solution)/shard_map/ppermute | solution.py:21
  65.8 2.3 reshape.188
  69.0 2.0 broadcast_multiply_fusion.3
  75.1 2.1 pad_maximum_fusion
  77.2 1.8 copy.13
  78.9 4.4 %reshape.195 = bf16[270,3072]{1,0:T(8,128)(2,1)} reshape(bf16[270,4,6,128]{3,2,1,0:T(8,128)(2,1)} %copy.13) | data formatting | bytes 3317760 | tf_op jit(solution)/shard_map/reshape | solution.py:113
  83.3 8.4 %fusion.8 = bf16[270,1152]{1,0:T(8,128)(2,1)} fusion(f32[270,1152]{1,0:T(8,128)} %fusion.3, bf16[1,1,1152,1152]{3,2,1,0:T(8,128)(2,1)S(1)} %copy-done, bf16[270,3072]{1,0:T(8,128)(2,1)} %reshape.195, bf16[3072,1152]{1,0:T(8,128)(2,1)} %bitcast.85), kind=kOutput, calls=%fused_computation.8 | convolution fusion | flops 2628599040 | bytes 13257216 | tf_op jit(solution)/shard_map/dot_general | solution.py:121
  91.7 3.5 convolution_multiply_fusion
  95.2 3.7 %fusion.11 = f32[2048,270]{1,0:T(8,128)S(1)} fusion(f32[270,270]{1,0:T(8,128)S(1)} %convolution_multiply_fusion, s32[270]{0:T(512)S(1)} %fusion.33), kind=kOutput, calls=%fused_computation.11 | convolution fusion | flops 1792143360 | bytes 2504520 | tf_op jit(solution)/shard_map/dot_general | solution.py:62
  98.9 16.6 %fusion.12 = f32[2048,2048]{1,0:T(8,128)} fusion(f32[2048,270]{1,0:T(8,128)S(1)} %fusion.11, s32[270]{0:T(512)S(1)} %reduce), kind=kOutput, calls=%fused_computation.12 | convolution fusion | flops 13590097920 | bytes 18990136 | tf_op jit(solution)/shard_map/dot_general | solution.py:69
  115.6 178.0 %reduce-scatter.3.cloned.1.call-done = f32[256,2048]{1,0:T(8,128)} async-done(((f32[2048,2048]{1,0:T(8,128)}), f32[256,2048]{1,0:T(8,128)}) %reduce-scatter.3.cloned.1.call-update) | async-done | bytes 2097168 | tf_op jit(solution)/shard_map/reduce_scatter | solution.py:31
  293.6 38.0 %reduce-scatter.5.cloned.1.call-done = f32[128,2048]{1,0:T(8,128)} async-done(((f32[256,2048]{1,0:T(8,128)}), f32[128,2048]{1,0:T(8,128)}) %reduce-scatter.5.cloned.1.call-update) | async-done | bytes 1048592 | tf_op jit(solution)/shard_map/reduce_scatter | solution.py:31
  331.6 23.3 %all_to_all.5 = f32[16,8,2048]{2,1,0:T(8,128)} all-to-all(f32[16,8,2048]{2,1,0:T(8,128)} %bitcast.83), channel_id=1, replica_groups=mesh['grp'=16,'sub_0'=8,'sub_1'=2] {'grp'}, dimensions={0} | all-to-all | bytes 2097152 | tf_op jit(solution)/shard_map/all_to_all | solution.py:42
  354.9 1.9 reduce_sum.9
  (59 shorter events, 23.8 us)
Async XLA Ops:
  6.5 16.7 %copy-start = (bf16[1,1,1152,1152]{3,2,1,0:T(8,128)(2,1)S(1)}, bf16[1,1,1152,1152]{3,2,1,0:T(8,128)(2,1)}, u32[]{:S(2)}) copy-start(bf16[1,1,1152,1152]{3,2,1,0:T(8,128)(2,1)} %param.9) | copy-start | bytes 7962628
  6.5 287.1 %reduce-scatter.3.cloned.1.call-start = ((), (), s32[]{:S(2)}) async-start(), calls=%async_computation.3 | async-start | bytes 18874368 | tf_op jit(solution)/shard_map/reduce_scatter | solution.py:31
  8.0 20.3 %collective-permute-start.2 = (s32[1,2,12]{2,1,0:T(2,128)}, s32[1,2,12]{2,1,0:T(2,128)}, u32[]{:S(2)}, u32[]{:S(2)}) collective-permute-start(s32[1,2,12]{2,1,0:T(2,128)} %get-tuple-element.7), channel_id=1, source_target_pairs={{0,16},{16,32},{32,48},{48,64},{64,80},{80,96},{96,112},{112,128},... | collective-permute-start | bytes 296 | tf_op jit(solution)/shard_map/ppermute | solution.py:21
  12.9 15.4 %collective-permute-start = (s32[1,2,12]{2,1,0:T(2,128)}, s32[1,2,12]{2,1,0:T(2,128)}, u32[]{:S(2)}, u32[]{:S(2)}) collective-permute-start(s32[1,2,12]{2,1,0:T(2,128)} %get-tuple-element.8), channel_id=1, source_target_pairs={{16,0},{32,16},{48,32},{64,48},{80,64},{96,80},{112,96},{128,112},... | collective-permute-start | bytes 296 | tf_op jit(solution)/shard_map/ppermute | solution.py:24
  28.3 9.1 %copy-start.1 = (bf16[270,9,128]{2,1,0:T(8,128)(2,1)S(1)}, bf16[270,9,128]{2,1,0:T(8,128)(2,1)}, u32[]{:S(2)}) copy-start(bf16[270,9,128]{2,1,0:T(8,128)(2,1)} %copy.9) | copy-start | bytes 1866244
  29.2 22.1 %collective-permute-start.4 = (s32[4,1,12]{2,1,0:T(1,128)S(1)}, s32[4,1,12]{2,1,0:T(1,128)S(1)}, u32[]{:S(2)}, u32[]{:S(2)}) collective-permute-start(s32[4,1,12]{2,1,0:T(1,128)S(1)} %get-tuple-element.5), channel_id=1, source_target_pairs={{1,0},{2,1},{3,2},{4,3},{5,4},{6,5},{7,6},{8,7},{9,8},{10,9},{11,1... | collective-permute-start | bytes 584 | tf_op jit(solution)/shard_map/ppermute | solution.py:24
  30.5 18.2 %collective-permute-start.6 = (s32[4,1,12]{2,1,0:T(1,128)S(1)}, s32[4,1,12]{2,1,0:T(1,128)S(1)}, u32[]{:S(2)}, u32[]{:S(2)}) collective-permute-start(s32[4,1,12]{2,1,0:T(1,128)S(1)} %get-tuple-element.6), channel_id=1, source_target_pairs={{0,1},{1,2},{2,3},{3,4},{4,5},{5,6},{6,7},{7,8},{8,9},{9,10},{10,1... | collective-permute-start | bytes 584 | tf_op jit(solution)/shard_map/ppermute | solution.py:21
  38.9 18.6 %collective-permute-start.3 = (bf16[270,768]{1,0:T(8,128)(2,1)S(1)}, bf16[270,768]{1,0:T(8,128)(2,1)}, u32[]{:S(2)}, u32[]{:S(2)}) collective-permute-start(bf16[270,768]{1,0:T(8,128)(2,1)S(1)} %bitcast.84), channel_id=1, source_target_pairs={{16,0},{32,16},{48,32},{64,48},{80,64},{96,80},{112,96},{128,112},... | collective-permute-start | bytes 1244168 | tf_op jit(solution)/shard_map/ppermute | solution.py:24
  40.8 25.0 %collective-permute-start.1 = (bf16[270,768]{1,0:T(8,128)(2,1)}, bf16[270,768]{1,0:T(8,128)(2,1)}, u32[]{:S(2)}, u32[]{:S(2)}) collective-permute-start(bf16[270,768]{1,0:T(8,128)(2,1)} %bitcast.26), channel_id=1, source_target_pairs={{0,16},{16,32},{32,48},{48,64},{64,80},{80,96},{96,112},{112,128},... | collective-permute-start | bytes 1244168 | tf_op jit(solution)/shard_map/ppermute | solution.py:21
  50.0 21.0 %collective-permute-start.7 = (bf16[270,768]{1,0:T(8,128)(2,1)}, bf16[270,768]{1,0:T(8,128)(2,1)}, u32[]{:S(2)}, u32[]{:S(2)}) collective-permute-start(bf16[270,768]{1,0:T(8,128)(2,1)} %bitcast.35), channel_id=1, source_target_pairs={{1,0},{2,1},{3,2},{4,3},{5,4},{6,5},{7,6},{8,7},{9,8},{10,9},{11,1... | collective-permute-start | bytes 1244168 | tf_op jit(solution)/shard_map/ppermute | solution.py:24
  51.7 16.4 %copy-start.5 = (bf16[6]{0:T(256)(128)(2,1)S(1)}, bf16[6]{0:T(256)(128)(2,1)}, u32[]{:S(2)}) copy-start(bf16[6]{0:T(256)(128)(2,1)} %compare_convert_fusion.2) | copy-start | bytes 40
  51.9 17.2 %copy-start.4 = (bf16[6]{0:T(256)(128)(2,1)S(1)}, bf16[6]{0:T(256)(128)(2,1)}, u32[]{:S(2)}) copy-start(bf16[6]{0:T(256)(128)(2,1)} %compare_convert_fusion.3) | copy-start | bytes 40
  52.7 20.7 %collective-permute-start.5 = (bf16[270,768]{1,0:T(8,128)(2,1)}, bf16[270,768]{1,0:T(8,128)(2,1)}, u32[]{:S(2)}, u32[]{:S(2)}) collective-permute-start(bf16[270,768]{1,0:T(8,128)(2,1)} %bitcast.32), channel_id=1, source_target_pairs={{0,1},{1,2},{2,3},{3,4},{4,5},{5,6},{6,7},{7,8},{8,9},{9,10},{10,1... | collective-permute-start | bytes 1244168 | tf_op jit(solution)/shard_map/ppermute | solution.py:21
  58.9 13.6 %copy-start.3 = (bf16[6]{0:T(256)(128)(2,1)S(1)}, bf16[6]{0:T(256)(128)(2,1)}, u32[]{:S(2)}) copy-start(bf16[6]{0:T(256)(128)(2,1)} %compare_convert_fusion) | copy-start | bytes 40
  69.0 5.9 %copy-start.2 = (bf16[6]{0:T(256)(128)(2,1)S(1)}, bf16[6]{0:T(256)(128)(2,1)}, u32[]{:S(2)}) copy-start(bf16[6]{0:T(256)(128)(2,1)} %compare_convert_fusion.1) | copy-start | bytes 40
  115.5 216.1 %reduce-scatter.5.cloned.1.call-start = ((), (), s32[]{:S(2)}) async-start(), calls=%async_computation.4 | async-start | bytes 3145728 | tf_op jit(solution)/shard_map/reduce_scatter | solution.py:31
Sparse Core Ops, SparseCore 0:
  115.6 177.9 reduce-scatter.2
  296.1 35.4 reduce-scatter.4
where the time goes:
time: 367 us; the launch traced here: 364 us
  waiting for transfers between devices  223 us (61%)
  matrix products  38 us (10%)
  starting transfers between devices  27.9 us (8%)
  blocking collectives  23.3 us (6%)
  local copies, waits for them, and re-layouts  23 us (6%)
  other arithmetic  14.9 us (4%)
  between operations  13.6 us (4%)
    reduce_scatter x2, waiting for transfers between devices, summed_rows(): shard = lax.psum_scatter(shard, axis, scatter_dimension=dim, tiled=True)  216 us
    all_to_all x1, blocking collectives, sum_at_owner(): pieces = lax.all_to_all(split_up(shard, dim, size), axis, 0, 0, tiled=True)  23.3 us
    ppermute x4, starting transfers between devices, extended(): lax.ppermute(lax.slice_in_dim(block, block.shape[dim] - width, None, axis...  21.4 us
    dot_general x1, matrix products, spread_block(): jnp.dot(placed_rows, col_table, precision=lax.Precision.HIGHEST, preferre...  16.6 us
    dot_general x1, matrix products, shards(): jnp.dot(margin, inverse_local, preferred_element_type=jnp.float32)  8.41 us
  transfers between devices with their start and end apart: 10, of which 3 were waited for; matrix products, arithmetic and copies ran while one was open for 8% of the time, Pallas kernels for 0%

commit v1 on v0

v1 whole, which is shorter than its diff:
```python
import functools

import jax
import jax.numpy as jnp
from jax import lax
from jax.experimental import pallas as pl
from jax.experimental.pallas import tpu as pltpu
from jax.sharding import PartitionSpec as P

K = 270
PANEL = 128
NB = 9
CMAX = 6
OWN = 8
KM = 256
KR = 16
LW = 128
WIDE = 384
DEEP = 256
XL = 2
CO = 2
MESH = pl.DeviceIdType.MESH
BF16 = jnp.bfloat16
F32 = jnp.float32


def sizes(mesh_shape):
    grp, sub = mesh_shape["grp"], mesh_shape["sub"]
    xh = 2 if grp >= 16 else 1
    return xh, grp // (xh * CO), sub // XL


def kernel(
    dims, basis, reqs, own, inv_h, stiff_h, coup_h, out,
    basisp, psend, rows, rreq, acc, base, coup, inv, stiff, total, ext, proj, ct, rtp, rt, rtr,
    orecv, xsend, xrecv, acc2, keep, sibs, sibr, zsend, zrecv,
    lsem, rqs, rqr, ps, pr, os_, or_, xs, xr, ss, sr, zs, zr,
):
    XH, Y, Z = dims
    Q = XH * Y * XL
    G, S = XH * Y * CO, Z * XL
    nco = OWN * G * S
    m1 = CO * Z * OWN
    kp = KM + KR
    width = NB * PANEL
    g, s = lax.axis_index("grp"), lax.axis_index("sub")
    xh, y, co = g // (Y * CO), (g // CO) % Y, g % CO
    z, xl = s // XL, s % XL
    has = [g > 0, g < G - 1, s > 0, s < S - 1]
    face = [(g - 1, s), (g + 1, s), (g, s - 1), (g, s + 1)]
    plane = []
    for k in range(Q):
        a, b, c = k // (Y * XL), (k // XL) % Y, k % XL
        plane.append((((xh + a) % XH * Y + (y + b) % Y) * CO + co, z * XL + (xl + c) % XL))
    sibling = (g + 1 - 2 * co, s)
    column = [(g, (z + k) % Z * XL + xl) for k in range(Z)]

    loads = [pltpu.make_async_copy(coup_h.at[d], coup.at[d], lsem.at[d]) for d in range(4)]
    loads.append(pltpu.make_async_copy(inv_h, inv, lsem.at[4]))
    loads.append(pltpu.make_async_copy(stiff_h, stiff, lsem.at[5]))

    barrier = pltpu.get_barrier_semaphore()
    for d in range(4):
        @pl.when(has[d])
        def _(d=d):
            pl.semaphore_signal(barrier, inc=1, device_id=face[d], device_id_type=MESH)
    for peer in plane[1:] + [sibling] + column[1:]:
        pl.semaphore_signal(barrier, inc=1, device_id=peer, device_id_type=MESH)
    for load in loads:
        load.start()

    basisp[KM:kp, :] = jnp.zeros((KR, width), BF16)
    basisp[0:K, :] = basis[...]
    for d in range(4):
        @pl.when(jnp.logical_not(has[d]))
        def _(d=d):
            for p in range(CMAX // 2):
                rows[d * (CMAX // 2) + p] = jnp.zeros((kp, 2 * PANEL), BF16)
    orecv[0] = own[0]

    faces = sum(h.astype(jnp.int32) for h in has)
    pl.semaphore_wait(barrier, faces + (Q - 1) + 1 + (Z - 1))

    def request(d):
        return pltpu.make_async_remote_copy(
            src_ref=reqs.at[d], dst_ref=rreq.at[d ^ 1], send_sem=rqs.at[d], recv_sem=rqr.at[d ^ 1],
            device_id=face[d], device_id_type=MESH)

    def request_in(d):
        return pltpu.make_async_remote_copy(
            src_ref=reqs.at[d], dst_ref=rreq.at[d], send_sem=rqs.at[d], recv_sem=rqr.at[d],
            device_id=face[d], device_id_type=MESH)

    def panels(d, p, into):
        n = CMAX // 2
        return pltpu.make_async_remote_copy(
            src_ref=psend.at[d * n + p], dst_ref=rows.at[into * n + p], send_sem=ps.at[d * n + p],
            recv_sem=pr.at[into * n + p], device_id=face[d], device_id_type=MESH)

    def owners(k):
        return pltpu.make_async_remote_copy(
            src_ref=own.at[0], dst_ref=orecv.at[k], send_sem=os_.at[k], recv_sem=or_.at[k],
            device_id=plane[k], device_id_type=MESH)

    def spread(k):
        return pltpu.make_async_remote_copy(
            src_ref=xsend.at[k], dst_ref=xrecv.at[k], send_sem=xs.at[k], recv_sem=xr.at[k],
            device_id=plane[k], device_id_type=MESH)

    def beside():
        return pltpu.make_async_remote_copy(
            src_ref=sibs, dst_ref=sibr, send_sem=ss.at[0], recv_sem=sr.at[0],
            device_id=sibling, device_id_type=MESH)

    def along(k):
        return pltpu.make_async_remote_copy(
            src_ref=zsend.at[k], dst_ref=zrecv.at[k], send_sem=zs.at[k], recv_sem=zr.at[k],
            device_id=column[k], device_id_type=MESH)

    order = (2, 3, 0, 1)
    for d in order:
        @pl.when(has[d])
        def _(d=d):
            request(d).start()
    for k in range(1, Q):
        owners(k).start()

    def own_rows(n, carry):
        at = pl.multiple_of(n * DEEP, DEEP)
        here = lax.broadcasted_iota(jnp.int32, (DEEP, KM + LW), 0) + at
        rtp[pl.ds(at, DEEP), :] = (own[1, 0:1, :] == here).astype(F32).astype(BF16)
        return carry

    acc[...] = jnp.zeros_like(acc)

    for p in range(CMAX // 2):
        for d in order:
            @pl.when(has[d])
            def _(d=d, p=p):
                if p == 0:
                    request_in(d).wait_recv()
                for h in range(2):
                    c = 2 * p + h
                    picked = None
                    for n in range(NB):
                        mark = (rreq[d, c : c + 1, :] == n).astype(F32).astype(BF16)
                        term = basisp[:, n * PANEL : (n + 1) * PANEL] * mark
                        picked = term if picked is None else picked + term
                    psend[d * (CMAX // 2) + p, :, h * PANEL : (h + 1) * PANEL] = picked
                panels(d, p, d ^ 1).start()

    lax.fori_loop(0, nco // DEEP, own_rows, 0)
    proj[...] = jnp.zeros_like(proj)

    for k in range(1, Q):
        owners(k).wait_recv()
    packed = []
    for first in range(0, Q, LW // KR):
        line = None
        for k in range(first, min(Q, first + LW // KR)):
            piece = orecv[k, :, KM : KM + LW]
            shift = (k - first) * KR
            piece = pltpu.roll(piece, shift, 1) if shift else piece
            line = piece if line is None else line + piece
        packed.append(line[0:1, :])

    def tables(n, carry):
        at = pl.multiple_of(n * DEEP, DEEP)
        here = lax.broadcasted_iota(jnp.int32, (DEEP, KM), 0) + at
        for k in range(Q):
            rt[pl.ds(at, DEEP), k * KM : (k + 1) * KM] = (
                (orecv[k, 0:1, 0:KM] == here).astype(F32).astype(BF16))
        narrow = lax.broadcasted_iota(jnp.int32, (DEEP, LW), 0) + at
        for i, line in enumerate(packed):
            rtr[pl.ds(at, DEEP), i * LW : (i + 1) * LW] = (line == narrow).astype(F32).astype(BF16)
        return carry

    lax.fori_loop(0, nco // DEEP, tables, 0)

    loads[4].wait()

    def inner(n, carry):
        at = pl.ds(pl.multiple_of(n * WIDE, WIDE), WIDE)
        base[:, at] = jnp.dot(basisp[...], inv[:, at], preferred_element_type=F32)
        return carry

    lax.fori_loop(0, width // WIDE, inner, 0)
    for d in range(4):
        loads[d].wait()
    for p in range(CMAX // 2):
        for d in (0, 1, 2, 3):
            i = d * (CMAX // 2) + p

            @pl.when(has[d])
            def _(d=d, p=p):
                panels(d, p, d).wait_recv()

            def margin(n, carry, d=d, p=p, i=i):
                at = pl.ds(pl.multiple_of(n * WIDE, WIDE), WIDE)
                acc[:, at] += jnp.dot(
                    rows[i], coup[d, 2 * PANEL * p : 2 * PANEL * (p + 1), at],
                    preferred_element_type=F32)
                return carry

            lax.fori_loop(0, width // WIDE, margin, 0)

    loads[5].wait()
    total[...] = acc[...].astype(BF16)

    def extend(n, carry):
        at = pl.ds(pl.multiple_of(n * WIDE, WIDE), WIDE)
        outer = jnp.dot(total[...], inv[:, at], preferred_element_type=F32)
        ext[:, at] = (base[:, at] + outer).astype(BF16)
        return carry

    lax.fori_loop(0, width // WIDE, extend, 0)

    def project(n, carry):
        at = pl.ds(pl.multiple_of(n * WIDE, WIDE), WIDE)
        proj[0:kp, at] = jnp.dot(ext[...], stiff[:, at], preferred_element_type=F32).astype(BF16)
        return carry

    lax.fori_loop(0, width // WIDE, project, 0)
    scale = float(width * K) ** (-0.5)
    ct[...] = (
        lax.dot_general(ext[...], proj[...], (((1,), (1,)), ((), ())), preferred_element_type=F32)
        * scale
    ).astype(BF16)

    for k in list(range(Q - 1, 0, -1)) + [0]:
        xsend[k] = lax.dot_general(
            ct[...], rtp[k * m1 : (k + 1) * m1, :], (((1,), (1,)), ((), ())),
            preferred_element_type=F32).astype(BF16)
        if k:
            spread(k).start()
    xrecv[0] = xsend[0]

    def add(table, lanes, block, first):
        def step(n, carry):
            at = pl.ds(pl.multiple_of(n * DEEP, DEEP), DEEP)
            term = jnp.dot(table[at, lanes], block, preferred_element_type=F32)
            acc2[at, :] = term if first else acc2[at, :] + term
            return carry

        lax.fori_loop(0, nco // DEEP, step, 0)

    for k in [0] + list(range(Q - 1, 0, -1)):
        if k:
            spread(k).wait_recv()
        add(rt, slice(k * KM, (k + 1) * KM), xrecv[k, 0:KM, :], k == 0)
    rest = jnp.concatenate([xrecv[k, KM:kp, :] for k in range(Q)], axis=0)
    if rtr.shape[1] > Q * KR:
        rest = jnp.concatenate([rest, jnp.zeros((rtr.shape[1] - Q * KR, m1), BF16)], axis=0)
    add(rtr, slice(0, rtr.shape[1]), rest, False)

    half = m1 // 2
    for n in range(nco // DEEP):
        at = slice(n * DEEP, (n + 1) * DEEP)
        turned = jnp.transpose(acc2[at, :])
        keep[:, at] = turned[0:half, :]
        sibs[:, at] = turned[half:, :]
    beside().start()
    beside().wait_recv()
    keep[...] += sibr[...]
    mid = nco // 2
    for k in range(1, Z):
        piece = keep[k * OWN : (k + 1) * OWN, :]
        zsend[k] = jnp.concatenate([piece[:, :mid], piece[:, mid:]], axis=0).astype(BF16)
        along(k).start()
    result = jnp.concatenate([keep[0:OWN, :mid], keep[0:OWN, mid:]], axis=0)
    for k in range(1, Z):
        along(k).wait_recv()
        result = result + zrecv[k].astype(F32)
    out[:, :mid] = result[0:OWN, :]
    out[:, mid:] = result[OWN:, :]

    for d in range(4):
        @pl.when(has[d])
        def _(d=d):
            request(d).wait_send()
            for p in range(CMAX // 2):
                panels(d, p, d ^ 1).wait_send()
    for k in range(1, Q):
        owners(k).wait_send()
        spread(k).wait_send()
    beside().wait_send()
    for k in range(1, Z):
        along(k).wait_send()


def shards(dims, basis, stiffness, inverse, coupling, panel_index, panel_count, owner_map):
    XH, Y, Z = dims
    Q = XH * Y * XL
    nco = OWN * XH * Y * CO * Z * XL
    m1 = CO * Z * OWN
    kp = KM + KR
    width = NB * PANEL
    g, s = lax.axis_index("grp"), lax.axis_index("sub")
    slots = jnp.arange(8, dtype=jnp.int32)
    wanted = jnp.pad(panel_index[0, 0], ((0, 0), (0, 8 - CMAX)))
    wanted = jnp.where(slots[None, :] < panel_count[0, 0][:, None], wanted, -1)
    reqs = jnp.broadcast_to(wanted[:, :, None], (4, 8, PANEL))

    m = owner_map[0, 0]
    mg, ms = m // (OWN * XL * Z), (m // OWN) % (XL * Z)
    a = (mg // (Y * CO) - g // (Y * CO)) % XH
    b = ((mg // CO) % Y - (g // CO) % Y) % Y
    c = (ms % XL - s % XL) % XL
    side = (mg % CO - g % CO) % CO
    up = (ms // XL - s // XL) % Z
    place = ((((a * Y + b) * XL + c) * CO + side) * Z + up) * OWN + m % OWN
    lines = jnp.stack([m, place])
    lines = jnp.pad(lines, ((0, 0), (0, kp - K)), constant_values=-1)
    lines = jnp.pad(lines, ((0, 0), (0, KM + LW - kp)))
    own = jnp.broadcast_to(lines[:, None, :], (2, 8, KM + LW))

    n = CMAX // 2
    packed = -(-Q * KR // LW) * LW
    vmem = pl.BlockSpec(memory_space=pltpu.VMEM)
    hbm = pl.BlockSpec(memory_space=pl.ANY)
    dma = pltpu.SemaphoreType.DMA
    return pl.pallas_call(
        functools.partial(kernel, dims),
        out_shape=jax.ShapeDtypeStruct((OWN, nco), F32),
        in_specs=[vmem, vmem, vmem, hbm, hbm, hbm],
        out_specs=vmem,
        scratch_shapes=[
            pltpu.VMEM((kp, width), BF16),
            pltpu.VMEM((4 * n, kp, 2 * PANEL), BF16),
            pltpu.VMEM((4 * n, kp, 2 * PANEL), BF16),
            pltpu.VMEM((4, 8, PANEL), jnp.int32),
            pltpu.VMEM((kp, width), F32),
            pltpu.VMEM((kp, width), F32),
            pltpu.VMEM((4, CMAX * PANEL, width), BF16),
            pltpu.VMEM((width, width), BF16),
            pltpu.VMEM((width, width), BF16),
            pltpu.VMEM((kp, width), BF16),
            pltpu.VMEM((kp, width), BF16),
            pltpu.VMEM((KM + LW, width), BF16),
            pltpu.VMEM((kp, KM + LW), BF16),
            pltpu.VMEM((nco, KM + LW), BF16),
            pltpu.VMEM((nco, Q * KM), BF16),
            pltpu.VMEM((nco, packed), BF16),
            pltpu.VMEM((Q, 8, KM + LW), jnp.int32),
            pltpu.VMEM((Q, kp, m1), BF16),
            pltpu.VMEM((Q, kp, m1), BF16),
            pltpu.VMEM((nco, m1), F32),
            pltpu.VMEM((m1 // 2, nco), F32),
            pltpu.VMEM((m1 // 2, nco), F32),
            pltpu.VMEM((m1 // 2, nco), F32),
            pltpu.VMEM((Z, 2 * OWN, nco // 2), BF16),
            pltpu.VMEM((Z, 2 * OWN, nco // 2), BF16),
            dma((6,)), dma((4,)), dma((4,)), dma((4 * n,)), dma((4 * n,)),
            dma((Q,)), dma((Q,)), dma((Q,)), dma((Q,)), dma((1,)), dma((1,)), dma((Z,)), dma((Z,)),
        ],
        compiler_params=pltpu.CompilerParams(
            collective_id=0, has_side_effects=True, vmem_limit_bytes=58 * 2**20
        ),
    )(basis[0, 0], reqs, own, inverse[0, 0], stiffness[0, 0], coupling[0, 0])


def solution(mesh):
    in_specs = (
        P("grp", "sub", None, None),
        P("grp", "sub", None, None),
        P("grp", "sub", None, None),
        P("grp", "sub", None, None, None),
        P("grp", "sub", None, None),
        P("grp", "sub", None),
        P("grp", "sub", None),
    )
    return jax.shard_map(
        functools.partial(shards, sizes(mesh.shape)),
        mesh=mesh, in_specs=in_specs, out_specs=P(("grp", "sub"), None), check_vma=False,
    )
```

time: 367 us -> 90.8 us (0.25)
  waiting for transfers between devices: 223 us -> 0 us
  Pallas kernels: 0 us -> 85.6 us
  matrix products: 38 us -> 0 us
  starting transfers between devices: 27.9 us -> 0 us
  blocking collectives: 23.3 us -> 0 us
  local copies, waits for them, and re-layouts: 23 us -> 2.75 us
  between operations: 13.6 us -> 0.01 us
  other arithmetic: 14.9 us -> 2.22 us
    reduce_scatter x2 -> x0, waiting for transfers between devices: 216 us -> none  [summed_rows(): shard = lax.psum_scatter(shard, axis, scatter_dimension=dim, tiled=True)]
    pallas_call x0 -> x1, Pallas kernels: none -> 85.6 us  [shards(): pl.pallas_call(functools.partial(kernel, dims), out_shape=jax.ShapeDtypeS...]
    dot_general x9 -> x0, matrix products: 38 us -> none  [the longest x1 16.6 us: spread_block(): jnp.dot(placed_rows, col_table, precision=lax.Precision.HIGHEST, preferre...]
    ppermute x8 -> x0, starting transfers between devices: 27.8 us -> none  [the longest x4 21.4 us: extended(): lax.ppermute(lax.slice_in_dim(block, block.shape[dim] - width, None, axis...]
    all_to_all x1 -> x0, blocking collectives: 23.3 us -> none  [sum_at_owner(): pieces = lax.all_to_all(split_up(shard, dim, size), axis, 0, 0, tiled=True)]
    reshape x5 -> x0, local copies, waits for them, and re-layouts: 11.1 us -> none  [the longest x4 6.75 us: live_slots(): return values.reshape(K, CMAX, PANEL) * alive_mask[None, :, None]]
    ppermute x8 -> x0, waiting for transfers between devices: 6.89 us -> none  [the longest x4 6.88 us: extended(): lax.ppermute(lax.slice_in_dim(block, block.shape[dim] - width, None, axis...]
    convert_element_type x4 -> x0, other arithmetic: 4.74 us -> none  [live_slots(): alive_mask = (jnp.arange(CMAX) < live_count).astype(values.dtype)]
  transfers between devices with their start and end apart: 10 -> 0, of which waited for: 3 -> 0; matrix products, arithmetic and copies ran while one was open for 8% -> 0% of each run, Pallas kernels for 0% -> 0%
where the time goes in v1:
time: 90.8 us; the launch traced here: 90.6 us
  Pallas kernels  85.6 us (94%)
  local copies, waits for them, and re-layouts  2.75 us (3%)
  other arithmetic  2.22 us (2%)
    pallas_call x1, Pallas kernels, shards(): pl.pallas_call(functools.partial(kernel, dims), out_shape=jax.ShapeDtypeS...  85.6 us

profile of v1, /device:TPU:25, one launch (start us, length us, event | category | flops | bytes accessed | tf_op | source)
XLA Modules:
  0.0 90.6 jit_solution(9737170167376380618)
XLA Ops:
  0.0 0.8 fusion.4
  0.8 0.7 pad_add_fusion
  1.5 0.8 pad_select_fusion
  2.2 0.7 broadcast_in_dim.9.reqs
  2.9 0.6 broadcast_in_dim.10.own
  3.5 85.6 %shard_map.73 = f32[8,2048]{1,0:T(8,128)} custom-call(bf16[270,1152]{1,0:T(8,128)(2,1)} %bitcast.11, s32[4,8,128]{2,1,0:T(8,128)} %broadcast_in_dim.9.reqs, s32[2,8,384]{2,1,0:T(8,128)} %broadcast_in_dim.10.own, bf16[1152,1152]{1,0:T(8,128)(2,1)} %bitcast.9, bf16[1152,1152]{1,0:T(8,128)(2,1)} %bitcast.10, bf16[4,768,1152]{2,1,0:T(8,128)(2,1)} %bitcast.8), custom_call_target="tpu_custom_call" | custom-call | tf_op jit(solution)/shard_map/pallas_call | solution.py:322
  89.1 1.5 %copy.9 = f32[8,2048]{1,0:T(8,128)} copy(f32[8,2048]{1,0:T(8,128)} %shard_map.73) | data formatting | bytes 131072
  (1 shorter events, 0.0 us)

commit v2 on v1

--- a/solution.py
+++ b/solution.py
@@ -31,8 +31,8 @@
 
 
 def kernel(
-    dims, basis, reqs, own, inv_h, stiff_h, coup_h, out,
-    basisp, psend, rows, rreq, acc, base, coup, inv, stiff, total, ext, proj, ct, rtp, rt, rtr,
+    dims, basis, index, count, owner, inv_h, stiff_h, coup_h, out,
+    basisp, reqs, own, psend, rows, rreq, acc, base, coup, inv, stiff, total, ext, proj, ct, rtp, rt, rtr,
     orecv, xsend, xrecv, acc2, keep, sibs, sibr, zsend, zrecv,
     lsem, rqs, rqr, ps, pr, os_, or_, xs, xr, ss, sr, zs, zr,
 ):
@@ -76,7 +76,23 @@
         def _(d=d):
             for p in range(CMAX // 2):
                 rows[d * (CMAX // 2) + p] = jnp.zeros((kp, 2 * PANEL), BF16)
-    orecv[0] = own[0]
+    for d in range(4):
+        for c in range(CMAX):
+            wanted = jnp.where(c < count[0, d], index[d, c], -1)
+            reqs[d, c : c + 1, :] = jnp.full((1, LW), wanted, jnp.int32)
+    own[0] = jnp.zeros((8, KM + LW), jnp.int32)
+    own[0, 0:1, 0:K] = owner[...]
+    m = jnp.broadcast_to(own[0, 0:1, :], (8, KM + LW))
+    own[0] = m
+    orecv[0] = m
+    bits = [n.bit_length() - 1 for n in (XL, Z, CO, Y, XH)]
+    ms, mg = m >> 3, m >> (3 + bits[0] + bits[1])
+    there = ((mg >> (bits[2] + bits[3])) - xh) & (XH - 1)
+    there = (there << bits[3]) + (((mg >> bits[2]) - y) & (Y - 1))
+    there = (there << bits[0]) + ((ms - xl) & (XL - 1))
+    there = (there << bits[2]) + ((mg - co) & (CO - 1))
+    there = (there << bits[1]) + (((ms >> bits[0]) - z) & (Z - 1))
+    own[1] = (there << 3) + (m & 7)
 
     faces = sum(h.astype(jnp.int32) for h in has)
     pl.semaphore_wait(barrier, faces + (Q - 1) + 1 + (Z - 1))
@@ -143,7 +159,7 @@
                     c = 2 * p + h
                     picked = None
                     for n in range(NB):
-                        mark = (rreq[d, c : c + 1, :] == n).astype(F32).astype(BF16)
+                        mark = (rreq[d, c : c + 1, 0:PANEL] == n).astype(F32).astype(BF16)
                         term = basisp[:, n * PANEL : (n + 1) * PANEL] * mark
                         picked = term if picked is None else picked + term
                     psend[d * (CMAX // 2) + p, :, h * PANEL : (h + 1) * PANEL] = picked
@@ -195,32 +211,16 @@
             def _(d=d, p=p):
                 panels(d, p, d).wait_recv()
 
-            def margin(n, carry, d=d, p=p, i=i):
-                at = pl.ds(pl.multiple_of(n * WIDE, WIDE), WIDE)
-                acc[:, at] += jnp.dot(
-                    rows[i], coup[d, 2 * PANEL * p : 2 * PANEL * (p + 1), at],
-                    preferred_element_type=F32)
-                return carry
-
-            lax.fori_loop(0, width // WIDE, margin, 0)
+            acc[...] += jnp.dot(
+                rows[i], coup[d, 2 * PANEL * p : 2 * PANEL * (p + 1), :],
+                preferred_element_type=F32)
 
     loads[5].wait()
     total[...] = acc[...].astype(BF16)
 
-    def extend(n, carry):
-        at = pl.ds(pl.multiple_of(n * WIDE, WIDE), WIDE)
-        outer = jnp.dot(total[...], inv[:, at], preferred_element_type=F32)
-        ext[:, at] = (base[:, at] + outer).astype(BF16)
-        return carry
-
-    lax.fori_loop(0, width // WIDE, extend, 0)
-
-    def project(n, carry):
-        at = pl.ds(pl.multiple_of(n * WIDE, WIDE), WIDE)
-        proj[0:kp, at] = jnp.dot(ext[...], stiff[:, at], preferred_element_type=F32).astype(BF16)
-        return carry
-
-    lax.fori_loop(0, width // WIDE, project, 0)
+    outer = jnp.dot(total[...], inv[...], preferred_element_type=F32)
+    ext[...] = (base[...] + outer).astype(BF16)
+    proj[0:kp, :] = jnp.dot(ext[...], stiff[...], preferred_element_type=F32).astype(BF16)
     scale = float(width * K) ** (-0.5)
     ct[...] = (
         lax.dot_general(ext[...], proj[...], (((1,), (1,)), ((), ())), preferred_element_type=F32)
@@ -235,23 +235,25 @@
             spread(k).start()
     xrecv[0] = xsend[0]
 
-    def add(table, lanes, block, first):
-        def step(n, carry):
-            at = pl.ds(pl.multiple_of(n * DEEP, DEEP), DEEP)
-            term = jnp.dot(table[at, lanes], block, preferred_element_type=F32)
-            acc2[at, :] = term if first else acc2[at, :] + term
-            return carry
-
-        lax.fori_loop(0, nco // DEEP, step, 0)
-
-    for k in [0] + list(range(Q - 1, 0, -1)):
-        if k:
-            spread(k).wait_recv()
-        add(rt, slice(k * KM, (k + 1) * KM), xrecv[k, 0:KM, :], k == 0)
+    def spread_from(k):
+        return pltpu.make_async_remote_copy(
+            src_ref=xsend.at[k], dst_ref=xrecv.at[k], send_sem=xs.at[k], recv_sem=xr.at[k],
+            device_id=sibling, device_id_type=MESH)
+
+    acc2[...] = jnp.dot(rt[:, 0:KM], xrecv[0, 0:KM, :], preferred_element_type=F32)
+
+    def add(n, carry):
+        k = Q - n
+        spread_from(k).wait_recv()
+        lanes = pl.ds(pl.multiple_of(k * KM, KM), KM)
+        acc2[...] += jnp.dot(rt[:, lanes], xrecv[k, 0:KM, :], preferred_element_type=F32)
+        return carry
+
+    lax.fori_loop(1, Q, add, 0)
     rest = jnp.concatenate([xrecv[k, KM:kp, :] for k in range(Q)], axis=0)
     if rtr.shape[1] > Q * KR:
         rest = jnp.concatenate([rest, jnp.zeros((rtr.shape[1] - Q * KR, m1), BF16)], axis=0)
-    add(rtr, slice(0, rtr.shape[1]), rest, False)
+    acc2[...] += jnp.dot(rtr[...], rest, preferred_element_type=F32)
 
     half = m1 // 2
     for n in range(nco // DEEP):
@@ -295,40 +297,24 @@
     m1 = CO * Z * OWN
     kp = KM + KR
     width = NB * PANEL
-    g, s = lax.axis_index("grp"), lax.axis_index("sub")
-    slots = jnp.arange(8, dtype=jnp.int32)
-    wanted = jnp.pad(panel_index[0, 0], ((0, 0), (0, 8 - CMAX)))
-    wanted = jnp.where(slots[None, :] < panel_count[0, 0][:, None], wanted, -1)
-    reqs = jnp.broadcast_to(wanted[:, :, None], (4, 8, PANEL))
-
-    m = owner_map[0, 0]
-    mg, ms = m // (OWN * XL * Z), (m // OWN) % (XL * Z)
-    a = (mg // (Y * CO) - g // (Y * CO)) % XH
-    b = ((mg // CO) % Y - (g // CO) % Y) % Y
-    c = (ms % XL - s % XL) % XL
-    side = (mg % CO - g % CO) % CO
-    up = (ms // XL - s // XL) % Z
-    place = ((((a * Y + b) * XL + c) * CO + side) * Z + up) * OWN + m % OWN
-    lines = jnp.stack([m, place])
-    lines = jnp.pad(lines, ((0, 0), (0, kp - K)), constant_values=-1)
-    lines = jnp.pad(lines, ((0, 0), (0, KM + LW - kp)))
-    own = jnp.broadcast_to(lines[:, None, :], (2, 8, KM + LW))
-
     n = CMAX // 2
     packed = -(-Q * KR // LW) * LW
     vmem = pl.BlockSpec(memory_space=pltpu.VMEM)
+    smem = pl.BlockSpec(memory_space=pltpu.SMEM)
     hbm = pl.BlockSpec(memory_space=pl.ANY)
     dma = pltpu.SemaphoreType.DMA
     return pl.pallas_call(
         functools.partial(kernel, dims),
         out_shape=jax.ShapeDtypeStruct((OWN, nco), F32),
-        in_specs=[vmem, vmem, vmem, hbm, hbm, hbm],
+        in_specs=[vmem, smem, smem, vmem, hbm, hbm, hbm],
         out_specs=vmem,
         scratch_shapes=[
             pltpu.VMEM((kp, width), BF16),
+            pltpu.VMEM((4, 8, LW), jnp.int32),
+            pltpu.VMEM((2, 8, KM + LW), jnp.int32),
             pltpu.VMEM((4 * n, kp, 2 * PANEL), BF16),
             pltpu.VMEM((4 * n, kp, 2 * PANEL), BF16),
-            pltpu.VMEM((4, 8, PANEL), jnp.int32),
+            pltpu.VMEM((4, 8, LW), jnp.int32),
             pltpu.VMEM((kp, width), F32),
             pltpu.VMEM((kp, width), F32),
             pltpu.VMEM((4, CMAX * PANEL, width), BF16),
@@ -356,7 +342,7 @@
         compiler_params=pltpu.CompilerParams(
             collective_id=0, has_side_effects=True, vmem_limit_bytes=58 * 2**20
         ),
-    )(basis[0, 0], reqs, own, inverse[0, 0], stiffness[0, 0], coupling[0, 0])
+    )(basis[0, 0], panel_index[0, 0], panel_count[0], owner_map[0], inverse[0, 0], stiffness[0, 0], coupling[0, 0])
 
 
 def solution(mesh):

time: 90.8 us -> 71.3 us (0.79)
  Pallas kernels: 85.6 us -> 69.7 us
  other arithmetic: 2.22 us -> 0 us
  local copies, waits for them, and re-layouts: 2.75 us -> 1.47 us
    pallas_call x1, Pallas kernels: 85.6 us -> 69.7 us  [shards(): pl.pallas_call(functools.partial(kernel, dims), out_shape=jax.ShapeDtypeS...]
    broadcast_in_dim x2 -> x0, local copies, waits for them, and re-layouts: 1.28 us -> none  [the longest x1 0.67 us: shards(): reqs = jnp.broadcast_to(wanted[:, :, None], (4, 8, PANEL))]
where the time goes in v2:
time: 71.3 us; the launch traced here: 71.2 us
  Pallas kernels  69.7 us (98%)
  local copies, waits for them, and re-layouts  1.47 us (2%)
    pallas_call x1, Pallas kernels, shards(): pl.pallas_call(functools.partial(kernel, dims), out_shape=jax.ShapeDtypeS...  69.7 us
    unnamed x1, local copies, waits for them, and re-layouts  1.47 us

profile of v2, /device:TPU:25, one launch (start us, length us, event | category | flops | bytes accessed | tf_op | source)
XLA Modules:
  0.0 71.2 jit_solution(5043294028702780176)
XLA Ops:
  0.0 69.7 %shard_map.73 = f32[8,2048]{1,0:T(8,128)} custom-call(bf16[270,1152]{1,0:T(8,128)(2,1)} %bitcast.10, s32[4,6]{1,0:T(4,128)} %bitcast.11, s32[1,4]{1,0:T(1,128)} %bitcast.13, s32[1,270]{1,0:T(1,128)} %bitcast.12, bf16[1152,1152]{1,0:T(8,128)(2,1)} %bitcast.8, bf16[1152,1152]{1,0:T(8,128)(2,1)} %bitcast.9, bf16[4,768,1152]{2,1,0:T(8,128)(2,1)} %bitcast.7), custom_call_target="tpu_custom_call" | custom-call | tf_op jit(solution)/shard_map/pallas_call | solution.py:306
  69.7 1.5 %copy.9 = f32[8,2048]{1,0:T(8,128)} copy(f32[8,2048]{1,0:T(8,128)} %shard_map.73) | data formatting | bytes 131072

commit v3 on v2

--- a/solution.py
+++ b/solution.py
@@ -123,14 +123,15 @@
             src_ref=xsend.at[k], dst_ref=xrecv.at[k], send_sem=xs.at[k], recv_sem=xr.at[k],
             device_id=plane[k], device_id_type=MESH)
 
-    def beside():
-        return pltpu.make_async_remote_copy(
-            src_ref=sibs, dst_ref=sibr, send_sem=ss.at[0], recv_sem=sr.at[0],
+    def beside(h):
+        return pltpu.make_async_remote_copy(
+            src_ref=sibs.at[h], dst_ref=sibr.at[h], send_sem=ss.at[h], recv_sem=sr.at[h],
             device_id=sibling, device_id_type=MESH)
 
-    def along(k):
-        return pltpu.make_async_remote_copy(
-            src_ref=zsend.at[k], dst_ref=zrecv.at[k], send_sem=zs.at[k], recv_sem=zr.at[k],
+    def along(h, k):
+        i = h * Z + k
+        return pltpu.make_async_remote_copy(
+            src_ref=zsend.at[i], dst_ref=zrecv.at[i], send_sem=zs.at[i], recv_sem=zr.at[i],
             device_id=column[k], device_id_type=MESH)
 
     order = (2, 3, 0, 1)
@@ -227,10 +228,13 @@
         * scale
     ).astype(BF16)
 
-    for k in list(range(Q - 1, 0, -1)) + [0]:
-        xsend[k] = lax.dot_general(
-            ct[...], rtp[k * m1 : (k + 1) * m1, :], (((1,), (1,)), ((), ())),
+    for k in range(Q - 2, -1, -2):
+        pair = lax.dot_general(
+            ct[...], rtp[k * m1 : (k + 2) * m1, :], (((1,), (1,)), ((), ())),
             preferred_element_type=F32).astype(BF16)
+        xsend[k + 1] = pair[:, m1:]
+        spread(k + 1).start()
+        xsend[k] = pair[:, :m1]
         if k:
             spread(k).start()
     xrecv[0] = xsend[0]
@@ -255,26 +259,33 @@
         rest = jnp.concatenate([rest, jnp.zeros((rtr.shape[1] - Q * KR, m1), BF16)], axis=0)
     acc2[...] += jnp.dot(rtr[...], rest, preferred_element_type=F32)
 
-    half = m1 // 2
-    for n in range(nco // DEEP):
-        at = slice(n * DEEP, (n + 1) * DEEP)
-        turned = jnp.transpose(acc2[at, :])
-        keep[:, at] = turned[0:half, :]
-        sibs[:, at] = turned[half:, :]
-    beside().start()
-    beside().wait_recv()
-    keep[...] += sibr[...]
-    mid = nco // 2
-    for k in range(1, Z):
-        piece = keep[k * OWN : (k + 1) * OWN, :]
-        zsend[k] = jnp.concatenate([piece[:, :mid], piece[:, mid:]], axis=0).astype(BF16)
-        along(k).start()
-    result = jnp.concatenate([keep[0:OWN, :mid], keep[0:OWN, mid:]], axis=0)
-    for k in range(1, Z):
-        along(k).wait_recv()
-        result = result + zrecv[k].astype(F32)
-    out[:, :mid] = result[0:OWN, :]
-    out[:, mid:] = result[OWN:, :]
+    half, mid, quarter = m1 // 2, nco // 2, nco // 4
+    far = sorted(range(1, Z), key=lambda k: abs(2 * k - Z))
+    for h in range(2):
+        for n in range(0, mid, DEEP):
+            at = h * mid + n
+            turned = jnp.transpose(acc2[at : at + DEEP, :])
+            keep[:, at : at + DEEP] = turned[0:half, :]
+            sibs[h, :, n : n + DEEP] = turned[half:, :]
+        beside(h).start()
+    for h in range(2):
+        at = h * mid
+        beside(h).wait_recv()
+        keep[:, at : at + mid] += sibr[h]
+        for k in far:
+            piece = keep[k * OWN : (k + 1) * OWN, at : at + mid]
+            zsend[h * Z + k] = jnp.concatenate(
+                [piece[:, :quarter], piece[:, quarter:]], axis=0).astype(BF16)
+            along(h, k).start()
+    for h in range(2):
+        at = h * mid
+        piece = keep[0:OWN, at : at + mid]
+        result = jnp.concatenate([piece[:, :quarter], piece[:, quarter:]], axis=0)
+        for k in range(1, Z):
+            along(h, k).wait_recv()
+            result = result + zrecv[h * Z + k].astype(F32)
+        out[:, at : at + quarter] = result[0:OWN, :]
+        out[:, at + quarter : at + mid] = result[OWN:, :]
 
     for d in range(4):
         @pl.when(has[d])
@@ -285,9 +296,10 @@
     for k in range(1, Q):
         owners(k).wait_send()
         spread(k).wait_send()
-    beside().wait_send()
-    for k in range(1, Z):
-        along(k).wait_send()
+    for h in range(2):
+        beside(h).wait_send()
+        for k in range(1, Z):
+            along(h, k).wait_send()
 
 
 def shards(dims, basis, stiffness, inverse, coupling, panel_index, panel_count, owner_map):
@@ -332,12 +344,13 @@
             pltpu.VMEM((Q, kp, m1), BF16),
             pltpu.VMEM((nco, m1), F32),
             pltpu.VMEM((m1 // 2, nco), F32),
-            pltpu.VMEM((m1 // 2, nco), F32),
-            pltpu.VMEM((m1 // 2, nco), F32),
-            pltpu.VMEM((Z, 2 * OWN, nco // 2), BF16),
-            pltpu.VMEM((Z, 2 * OWN, nco // 2), BF16),
+            pltpu.VMEM((2, m1 // 2, nco // 2), F32),
+            pltpu.VMEM((2, m1 // 2, nco // 2), F32),
+            pltpu.VMEM((2 * Z, 2 * OWN, nco // 4), BF16),
+            pltpu.VMEM((2 * Z, 2 * OWN, nco // 4), BF16),
             dma((6,)), dma((4,)), dma((4,)), dma((4 * n,)), dma((4 * n,)),
-            dma((Q,)), dma((Q,)), dma((Q,)), dma((Q,)), dma((1,)), dma((1,)), dma((Z,)), dma((Z,)),
+            dma((Q,)), dma((Q,)), dma((Q,)), dma((Q,)), dma((2,)), dma((2,)),
+            dma((2 * Z,)), dma((2 * Z,)),
         ],
         compiler_params=pltpu.CompilerParams(
             collective_id=0, has_side_effects=True, vmem_limit_bytes=58 * 2**20

time: 71.3 us -> 70.2 us (0.985)
  Pallas kernels: 69.7 us -> 68.4 us
    pallas_call x1, Pallas kernels: 69.7 us -> 68.4 us  [shards(): pl.pallas_call(functools.partial(kernel, dims), out_shape=jax.ShapeDtypeS...]
where the time goes in v3:
time: 70.2 us; the launch traced here: 69.9 us
  Pallas kernels  68.4 us (97%)
  local copies, waits for them, and re-layouts  1.47 us (2%)
    pallas_call x1, Pallas kernels, shards(): pl.pallas_call(functools.partial(kernel, dims), out_shape=jax.ShapeDtypeS...  68.4 us
    unnamed x1, local copies, waits for them, and re-layouts  1.47 us

profile of v3, /device:TPU:25, one launch (start us, length us, event | category | flops | bytes accessed | tf_op | source)
XLA Modules:
  0.0 69.9 jit_solution(14255162759630415397)
XLA Ops:
  0.0 68.4 %shard_map.73 = f32[8,2048]{1,0:T(8,128)} custom-call(bf16[270,1152]{1,0:T(8,128)(2,1)} %bitcast.10, s32[4,6]{1,0:T(4,128)} %bitcast.11, s32[1,4]{1,0:T(1,128)} %bitcast.13, s32[1,270]{1,0:T(1,128)} %bitcast.12, bf16[1152,1152]{1,0:T(8,128)(2,1)} %bitcast.8, bf16[1152,1152]{1,0:T(8,128)(2,1)} %bitcast.9, bf16[4,768,1152]{2,1,0:T(8,128)(2,1)} %bitcast.7), custom_call_target="tpu_custom_call" | custom-call | tf_op jit(solution)/shard_map/pallas_call | solution.py:318
  68.4 1.5 %copy.9 = f32[8,2048]{1,0:T(8,128)} copy(f32[8,2048]{1,0:T(8,128)} %shard_map.73) | data formatting | bytes 131072

commit v4 on v3

--- a/solution.py
+++ b/solution.py
@@ -66,8 +66,6 @@
             pl.semaphore_signal(barrier, inc=1, device_id=face[d], device_id_type=MESH)
     for peer in plane[1:] + [sibling] + column[1:]:
         pl.semaphore_signal(barrier, inc=1, device_id=peer, device_id_type=MESH)
-    for load in loads:
-        load.start()
 
     basisp[KM:kp, :] = jnp.zeros((KR, width), BF16)
     basisp[0:K, :] = basis[...]
@@ -141,6 +139,8 @@
             request(d).start()
     for k in range(1, Q):
         owners(k).start()
+    for load in loads:
+        load.start()
 
     def own_rows(n, carry):
         at = pl.multiple_of(n * DEEP, DEEP)
@@ -257,14 +257,14 @@
     rest = jnp.concatenate([xrecv[k, KM:kp, :] for k in range(Q)], axis=0)
     if rtr.shape[1] > Q * KR:
         rest = jnp.concatenate([rest, jnp.zeros((rtr.shape[1] - Q * KR, m1), BF16)], axis=0)
-    acc2[...] += jnp.dot(rtr[...], rest, preferred_element_type=F32)
 
     half, mid, quarter = m1 // 2, nco // 2, nco // 4
     far = sorted(range(1, Z), key=lambda k: abs(2 * k - Z))
     for h in range(2):
         for n in range(0, mid, DEEP):
             at = h * mid + n
-            turned = jnp.transpose(acc2[at : at + DEEP, :])
+            last = jnp.dot(rtr[at : at + DEEP, :], rest, preferred_element_type=F32)
+            turned = jnp.transpose(acc2[at : at + DEEP, :] + last)
             keep[:, at : at + DEEP] = turned[0:half, :]
             sibs[h, :, n : n + DEEP] = turned[half:, :]
         beside(h).start()

time: 70.2 us -> 70.2 us (level)
  no operation moved by 1% of the time
where the time goes in v4:
time: 70.2 us; the launch traced here: 69.7 us
  Pallas kernels  68.3 us (97%)
  local copies, waits for them, and re-layouts  1.47 us (2%)
    pallas_call x1, Pallas kernels, shards(): pl.pallas_call(functools.partial(kernel, dims), out_shape=jax.ShapeDtypeS...  68.3 us
    unnamed x1, local copies, waits for them, and re-layouts  1.47 us

profile of v4, /device:TPU:25, one launch (start us, length us, event | category | flops | bytes accessed | tf_op | source)
XLA Modules:
  0.0 69.7 jit_solution(8801390897026068000)
XLA Ops:
  0.0 68.3 %shard_map.73 = f32[8,2048]{1,0:T(8,128)} custom-call(bf16[270,1152]{1,0:T(8,128)(2,1)} %bitcast.10, s32[4,6]{1,0:T(4,128)} %bitcast.11, s32[1,4]{1,0:T(1,128)} %bitcast.13, s32[1,270]{1,0:T(1,128)} %bitcast.12, bf16[1152,1152]{1,0:T(8,128)(2,1)} %bitcast.8, bf16[1152,1152]{1,0:T(8,128)(2,1)} %bitcast.9, bf16[4,768,1152]{2,1,0:T(8,128)(2,1)} %bitcast.7), custom_call_target="tpu_custom_call" | custom-call | tf_op jit(solution)/shard_map/pallas_call | solution.py:318
  68.3 1.5 %copy.9 = f32[8,2048]{1,0:T(8,128)} copy(f32[8,2048]{1,0:T(8,128)} %shard_map.73) | data formatting | bytes 131072
